TPU v7x, 32 devices: a whole 2x2x4 slice. The times are simulated.
32 devices in a mesh: ia: 4 (over z), ja: 4 (over y, x), ka: 2 (over core).
Axes of the slice: x: 2, y: 2, z: 4, core: 2. Of those that a mesh axis runs over, the one named last changes fastest.
Arguments:
- tensor: float32 [32, 1024, 1024], P('ka', 'ja', 'ia'), may hold values from -6 to 6
- factor_a: float32 [64, 1024], P('ka', 'ia'), may hold values from -4 to 4
- factor_b: float32 [64, 1024], P('ia', 'ja'), as said below
- factor_c: float32 [64, 32], P('ia', 'ka'), as said below
Outputs:
- gradient: float32 [64, 1024], P('ka', 'ia')
Inputs may be any that keep to these rules, and one draw needn't show every extreme that they name: `factor_b`: nonnegative entries. `factor_c`: nonnegative entries.
All inputs are finite; a program needn't handle non-finite values.
Results may differ from a plain program's by a relative error of at most 0.0001.
Values sent between devices are 32-bit elements; how exact they have to be, the bound alone decides.
A program may use at most 64 MiB of HBM per device.

v0:
```python
import jax
import jax.numpy as jnp
from jax import lax
from jax.sharding import PartitionSpec as P


def local(tensor, factor_a, factor_b, factor_c):
    highest = lax.Precision.HIGHEST
    rank_b, rank_c = (
        lax.all_gather(factor_b, "ia", axis=0, tiled=True),
        lax.all_gather(factor_c, "ia", axis=0, tiled=True),
    )
    inner = jnp.einsum(
        "rj,kji->rki", rank_b, tensor, preferred_element_type=jnp.float32, precision=highest
    )
    partial_value = jnp.einsum(
        "rki,rk->ri", inner, rank_c, preferred_element_type=jnp.float32, precision=highest
    )
    local_b = jnp.dot(rank_b, rank_b.T, preferred_element_type=jnp.float32, precision=highest)
    local_c = jnp.dot(rank_c, rank_c.T, preferred_element_type=jnp.float32, precision=highest)
    gram_c = lax.psum(local_c, "ka")
    share_rows = factor_a.shape[0]
    offset = lax.axis_index("ka") * share_rows
    gram_b = lax.psum(local_b, "ja")
    gram_rows = lax.dynamic_slice_in_dim(gram_b, offset, share_rows, 0)
    summed_all = lax.psum(partial_value, ("ja", "ka"))
    product = lax.dynamic_slice_in_dim(summed_all, offset, share_rows, 0)
    ranks_a = lax.all_gather(factor_a, "ka", axis=0, tiled=True)
    own_c = lax.dynamic_slice_in_dim(gram_c, offset, share_rows, 0)
    own_rows = gram_rows * own_c
    return product - jnp.dot(
        own_rows, ranks_a, preferred_element_type=jnp.float32, precision=highest
    )


def solution(mesh):
    in_specs = (P("ka", "ja", "ia"), P("ka", "ia"), P("ia", "ja"), P("ia", "ka"))
    out_specs = P("ka", "ia")
    return jax.shard_map(local, mesh=mesh, in_specs=in_specs, out_specs=out_specs, check_vma=False)
```

profile of v0, /device:TPU:0, one launch (start us, length us, event | category | flops | bytes accessed | tf_op | source)
XLA Modules:
  0.0 104.0 jit_solution(9680976829940590637)
XLA Ops:
  6.5 0.0 copy-start
  6.5 0.0 all-reduce.2.cloned.1.call-start
  6.5 15.2 %all_gather.9 = f32[64,256]{1,0:T(8,128)S(1)} all-gather(f32[16,256]{1,0:T(8,128)} %param.6), channel_id=1, replica_groups=mesh['ia'=4,'ja'=4,'ka'=2] {'ia'}, dimensions={0}, use_global_device_ids=true | all-gather | bytes 81920 | tf_op jit(solution)/shard_map/all_gather | solution.py:10
  21.8 13.3 %all_gather.10 = f32[64,16]{1,0:T(8,128)S(1)} all-gather(f32[16,16]{1,0:T(8,128)} %param.7), channel_id=1, replica_groups=mesh['ia'=4,'ja'=4,'ka'=2] {'ia'}, dimensions={0}, use_global_device_ids=true | all-gather | bytes 5120 | tf_op jit(solution)/shard_map/all_gather | solution.py:11
  35.1 4.8 %fusion.2 = f32[64,16,256]{2,0,1:T(8,128)S(1)} fusion(f32[16,256,256]{2,1,0:T(8,128)} %param.4, f32[64,256]{1,0:T(8,128)S(1)} %all_gather.9), kind=kOutput, calls=%fused_computation.3 | convolution fusion | flops 805306368 | bytes 5308416 | tf_op jit(solution)/shard_map/rj,kji->rki/dot_general | solution.py:13
  39.9 1.3 %fusion = f32[64,1,256]{2,1,0:T(1,128)S(1)} fusion(f32[64,16,1]{1,2,0:T(1,128)S(1)} %bitcast.16, f32[64,16,256]{2,0,1:T(8,128)S(1)} %fusion.2), kind=kOutput, calls=%fused_computation.1 | convolution fusion | flops 3145728 | bytes 1118208 | tf_op jit(solution)/shard_map/rki,rk->ri/dot_general | solution.py:16
  41.2 0.6 copy.11
  41.8 0.0 all-reduce.2.cloned.1.call-update
  41.8 0.2 fusion.8
  42.1 0.2 fusion.9
  42.2 16.3 %psum.22 = f32[64,64]{1,0:T(8,128)S(1)} all-reduce(f32[64,64]{1,0:T(8,128)S(1)} %fusion.8), channel_id=1, replica_groups=mesh['ia'=4,'ja'=4,'ka'=2] {'ja'}, use_global_device_ids=true, to_apply=%region_1.0 | all-reduce | flops 4096 | bytes 32768 | tf_op jit(solution)/shard_map/psum | solution.py:24
  58.6 3.4 %psum.23 = f32[64,64]{1,0:T(8,128)S(1)} all-reduce(f32[64,64]{1,0:T(8,128)S(1)} %fusion.9), channel_id=1, replica_groups=mesh['ia'=4,'ja'=4,'ka'=2] {'ka'}, use_global_device_ids=true, to_apply=%region_2.0 | all-reduce | flops 4096 | bytes 32768 | tf_op jit(solution)/shard_map/psum | solution.py:21
  62.0 0.0 copy-done
  62.0 1.9 %all_gather.11 = f32[64,256]{1,0:T(8,128)S(1)} all-gather(f32[32,256]{1,0:T(8,128)S(1)} %copy-done), channel_id=1, replica_groups=mesh['ia'=4,'ja'=4,'ka'=2] {'ka'}, dimensions={0}, use_global_device_ids=true | all-gather | bytes 98304 | tf_op jit(solution)/shard_map/all_gather | solution.py:28
  63.9 31.8 %all-reduce.2.cloned.1.call-done = f32[64,256]{1,0:T(8,128)} async-done(((f32[64,256]{1,0:T(8,128)}), f32[64,256]{1,0:T(8,128)}) %all-reduce.2.cloned.1.call-update) | async-done | bytes 65552 | tf_op jit(solution)/shard_map/psum | solution.py:26
  95.7 1.5 %convolution_subtract_fusion = f32[32,256]{1,0:T(8,128)} fusion(f32[64,256]{1,0:T(8,128)S(1)} %all_gather.11, f32[64,256]{1,0:T(8,128)} %all-reduce.2.cloned.1.call-done, s32[]{:T(128)S(6)} %select_n.2, f32[64,64]{1,0:T(8,128)S(1)} %psum.23, f32[64,64]{1,0:T(8,128)S(1)} %psum.22), kind=kOutput, calls=%fused_computation | convolution fusion | flops 6301696 | bytes 164864 | tf_op jit(solution)/shard_map/dot_general | solution.py:31
Async XLA Ops:
  6.5 55.5 %copy-start = (f32[32,256]{1,0:T(8,128)S(1)}, f32[32,256]{1,0:T(8,128)}, u32[]{:S(2)}) copy-start(f32[32,256]{1,0:T(8,128)} %param.5) | copy-start | bytes 98308
  6.5 89.1 %all-reduce.2.cloned.1.call-start = ((), (), s32[]{:S(2)}) async-start(), calls=%async_computation | async-start | bytes 131072 | tf_op jit(solution)/shard_map/psum | solution.py:26
Sparse Core Ops, SparseCore 0:
  42.0 53.6 all-reduce.1
where the time goes:
time: 104 us
  blocking collectives  50.1 us (48%)
  waiting for transfers between devices  31.8 us (31%)
  between operations  13.4 us (13%)
  matrix products  8.04 us (8%)
    psum x1, waiting for transfers between devices, local(): summed_all = lax.psum(partial_value, ('ja', 'ka'))  31.8 us
    psum x1, blocking collectives, local(): gram_b = lax.psum(local_b, 'ja')  16.3 us
    all_gather x1, blocking collectives, local(): lax.all_gather(factor_b, 'ia', axis=0, tiled=True)  15.2 us
    all_gather x1, blocking collectives, local(): lax.all_gather(factor_c, 'ia', axis=0, tiled=True)  13.3 us
    dot_general x1, matrix products, local(): jnp.einsum('rj,kji->rki', rank_b, tensor, preferred_element_type=jnp.floa...  4.8 us
    psum x1, blocking collectives, local(): gram_c = lax.psum(local_c, 'ka')  3.41 us
  transfers between devices with their start and end apart: 1, of which 1 were waited for; matrix products, arithmetic and copies ran while one was open for 0% of the time, Pallas kernels for 0%

commit v1 on v0

v1 whole, which is shorter than its diff:
```python
import functools

import jax
import jax.numpy as jnp
from jax import lax
from jax.experimental import pallas as pl
from jax.experimental.pallas import tpu as pltpu
from jax.sharding import PartitionSpec as P

MESH = pl.DeviceIdType.MESH
F32 = jnp.float32
BF16 = jnp.bfloat16
NN = (((1,), (0,)), ((), ()))
NT = (((1,), (1,)), ((), ()))


def split(x):
    high = x.astype(BF16)
    return high, (x - high.astype(F32)).astype(BF16)


def dot(x, y, dims=NN):
    return lax.dot_general(x, y, dims, preferred_element_type=F32)


def dot3(x, y, dims=NN):
    xh, xl = split(x)
    yh, yl = split(y)
    return dot(xh, yh, dims) + (dot(xh, yl, dims) + dot(xl, yh, dims))


def kernel(
    n_ia, n_ja, n_ka, groups,
    t_hbm, a_hbm, b_hbm, c_hbm, out_ref,
    t_v, th, tl, pack, c_v, a_v, gc, part, recv,
    t_sem, loc_sem, pack_send, pack_recv, gc_send, gc_recv,
    rs_send, rs_recv, ag_send, ag_recv,
):
    ia, ja, ka = lax.axis_index("ia"), lax.axis_index("ja"), lax.axis_index("ka")
    planes, jl, il = t_v.shape
    rb = pack.shape[1]
    ranks = rb * n_ia
    ra = a_v.shape[1]
    rows = part.shape[1]
    n_red = n_ja * n_ka
    me = ja * n_ka + ka
    step = planes // groups

    own_b = pltpu.make_async_copy(b_hbm, pack.at[ia, :, pl.ds(0, jl)], loc_sem.at[0])
    own_c = pltpu.make_async_copy(c_hbm, c_v, loc_sem.at[1])
    own_b.start()
    own_c.start()
    loads = []
    for g in range(groups):
        load = pltpu.make_async_copy(
            t_hbm.at[pl.ds(g * step, step)], t_v.at[pl.ds(g * step, step)], t_sem.at[g]
        )
        load.start()
        loads.append(load)
    a_v[...] = jnp.zeros_like(a_v)
    own_a = pltpu.make_async_copy(a_hbm, a_v.at[ka], loc_sem.at[2])
    own_a.start()

    barrier = pltpu.get_barrier_semaphore()
    for d in range(1, n_ia):
        pl.semaphore_signal(
            barrier, inc=1, device_id={"ia": lax.rem(ia + d, n_ia)}, device_id_type=MESH
        )
    for d in range(1, n_red):
        peer = lax.rem(me + d, n_red)
        pl.semaphore_signal(
            barrier, inc=1, device_id={"ja": peer // n_ka, "ka": lax.rem(peer, n_ka)},
            device_id_type=MESH,
        )
    own_c.wait()
    pack[ia, :, jl:] = jnp.concatenate(
        [c_v[...], jnp.zeros((rb, pack.shape[2] - jl - planes), F32)], axis=1
    )
    own_b.wait()
    pl.semaphore_wait(barrier, n_ia - 1 + n_red - 1)

    gathers = []
    for d in range(1, n_ia):
        copy = pltpu.make_async_remote_copy(
            src_ref=pack.at[ia], dst_ref=pack.at[ia],
            send_sem=pack_send.at[d - 1], recv_sem=pack_recv.at[ia],
            device_id={"ia": lax.rem(ia + d, n_ia)}, device_id_type=MESH,
        )
        copy.start()
        gathers.append(copy)

    for g in range(groups):
        loads[g].wait()

        @pl.loop(g * step, (g + 1) * step)
        def _(k):
            high, low = split(t_v[k])
            th[k] = high
            tl[k] = low

    for d in range(1, n_ia):
        q = lax.rem(ia + n_ia - d, n_ia)
        pltpu.make_async_remote_copy(
            src_ref=pack.at[q], dst_ref=pack.at[q],
            send_sem=pack_send.at[d - 1], recv_sem=pack_recv.at[q],
            device_id={"ia": q}, device_id_type=MESH,
        ).wait_recv()
    both = jnp.concatenate([pack[q] for q in range(n_ia)], axis=0)
    rank_b = both[:, :jl]
    rank_c = both[:, jl:]

    gc[ka] = dot3(rank_c, rank_c, NT)
    grams = []
    for d in range(1, n_ka):
        copy = pltpu.make_async_remote_copy(
            src_ref=gc.at[ka], dst_ref=gc.at[ka],
            send_sem=gc_send.at[d - 1], recv_sem=gc_recv.at[ka],
            device_id={"ka": lax.rem(ka + d, n_ka)}, device_id_type=MESH,
        )
        copy.start()
        grams.append(copy)

    bh, bl = split(rank_b)
    lhs = jnp.concatenate([bh, bl], axis=0)
    total = jnp.zeros((ranks, il), F32)
    for k in range(planes):
        wide = dot(lhs, th[k])
        inner = wide[:ranks] + (wide[ranks:] + dot(bh, tl[k]))
        total = total + inner * rank_c[:, k : k + 1]
    narrow = dot(lhs, bh, NT)
    gram_b = narrow[:ranks] + (narrow[ranks:] + dot(bh, bl, NT))

    own_a.wait()
    for d in range(1, n_ka):
        q = lax.rem(ka + n_ka - d, n_ka)
        pltpu.make_async_remote_copy(
            src_ref=gc.at[q], dst_ref=gc.at[q],
            send_sem=gc_send.at[d - 1], recv_sem=gc_recv.at[q],
            device_id={"ka": q}, device_id_type=MESH,
        ).wait_recv()
    gram_c = gc[0]
    for q in range(1, n_ka):
        gram_c = gram_c + gc[q]
    share = jnp.concatenate([a_v[q] for q in range(n_ka)], axis=0)
    total = total - dot3(gram_b * gram_c, share)

    for kk in range(n_ka):
        for jj in range(n_ja):
            low = kk * ra + jj * rows
            part[jj * n_ka + kk] = total[low : low + rows]
    scatters = []
    for d in range(1, n_red):
        peer = lax.rem(me + d, n_red)
        copy = pltpu.make_async_remote_copy(
            src_ref=part.at[peer], dst_ref=recv.at[me],
            send_sem=rs_send.at[d - 1], recv_sem=rs_recv.at[me],
            device_id={"ja": peer // n_ka, "ka": lax.rem(peer, n_ka)}, device_id_type=MESH,
        )
        copy.start()
        scatters.append(copy)
    summed = part[me]
    for d in range(1, n_red):
        q = lax.rem(me + n_red - d, n_red)
        pltpu.make_async_remote_copy(
            src_ref=part.at[q], dst_ref=recv.at[q],
            send_sem=rs_send.at[d - 1], recv_sem=rs_recv.at[q],
            device_id={"ja": q // n_ka, "ka": lax.rem(q, n_ka)}, device_id_type=MESH,
        ).wait_recv()
        summed = summed + recv[q]

    out_ref[ja] = summed
    spreads = []
    for d in range(1, n_ja):
        copy = pltpu.make_async_remote_copy(
            src_ref=out_ref.at[ja], dst_ref=out_ref.at[ja],
            send_sem=ag_send.at[d - 1], recv_sem=ag_recv.at[ja],
            device_id={"ja": lax.rem(ja + d, n_ja)}, device_id_type=MESH,
        )
        copy.start()
        spreads.append(copy)
    for copy in gathers + grams + scatters:
        copy.wait_send()
    for d in range(1, n_ja):
        q = lax.rem(ja + n_ja - d, n_ja)
        pltpu.make_async_remote_copy(
            src_ref=out_ref.at[q], dst_ref=out_ref.at[q],
            send_sem=ag_send.at[d - 1], recv_sem=ag_recv.at[q],
            device_id={"ja": q}, device_id_type=MESH,
        ).wait_recv()
    for copy in spreads:
        copy.wait_send()


def local(sizes, tensor, factor_a, factor_b, factor_c):
    n_ia, n_ja, n_ka = sizes
    planes, jl, il = tensor.shape
    ra, rb = factor_a.shape[0], factor_b.shape[0]
    ranks = rb * n_ia
    rows = ra // n_ja
    n_red = n_ja * n_ka
    groups = 4 if planes % 4 == 0 else 1
    wide_c = -(-planes // 128) * 128
    dma = pltpu.SemaphoreType.DMA
    out = pl.pallas_call(
        functools.partial(kernel, n_ia, n_ja, n_ka, groups),
        out_shape=jax.ShapeDtypeStruct((n_ja, rows, il), F32),
        in_specs=[pl.BlockSpec(memory_space=pl.ANY)] * 4,
        out_specs=pl.BlockSpec(memory_space=pltpu.VMEM),
        scratch_shapes=[
            pltpu.VMEM((planes, jl, il), F32),
            pltpu.VMEM((planes, jl, il), BF16),
            pltpu.VMEM((planes, jl, il), BF16),
            pltpu.VMEM((n_ia, rb, jl + wide_c), F32),
            pltpu.VMEM((rb, planes), F32),
            pltpu.VMEM((n_ka, ra, il), F32),
            pltpu.VMEM((n_ka, ranks, ranks), F32),
            pltpu.VMEM((n_red, rows, il), F32),
            pltpu.VMEM((n_red, rows, il), F32),
            dma((groups,)),
            dma((3,)),
            dma((n_ia,)),
            dma((n_ia,)),
            dma((n_ka,)),
            dma((n_ka,)),
            dma((n_red,)),
            dma((n_red,)),
            dma((n_ja,)),
            dma((n_ja,)),
        ],
        compiler_params=pltpu.CompilerParams(
            collective_id=0, has_side_effects=True, vmem_limit_bytes=56 * 2**20
        ),
        cost_estimate=pl.CostEstimate(
            flops=6 * ranks * planes * jl * il,
            bytes_accessed=4 * planes * jl * il,
            transcendentals=0,
        ),
    )(tensor, factor_a, factor_b, factor_c)
    return out.reshape(ra, il)


def solution(mesh):
    sizes = tuple(mesh.shape[name] for name in ("ia", "ja", "ka"))
    in_specs = (P("ka", "ja", "ia"), P("ka", "ia"), P("ia", "ja"), P("ia", "ka"))
    return jax.shard_map(
        functools.partial(local, sizes), mesh=mesh, in_specs=in_specs,
        out_specs=P("ka", "ia"), check_vma=False,
    )
```

time: 104 us -> 19.7 us (0.19)
  blocking collectives: 50.1 us -> 0 us
  waiting for transfers between devices: 31.8 us -> 0 us
  Pallas kernels: 0 us -> 18.1 us
  between operations: 13.4 us -> 0.01 us
  matrix products: 8.04 us -> 0 us
    psum x1 -> x0, waiting for transfers between devices: 31.8 us -> none  [local(): summed_all = lax.psum(partial_value, ('ja', 'ka'))]
    all_gather x3 -> x0, blocking collectives: 30.4 us -> none  [the longest x1 15.2 us: local(): lax.all_gather(factor_b, 'ia', axis=0, tiled=True)]
    psum x2 -> x0, blocking collectives: 19.7 us -> none  [the longest x1 16.3 us: local(): gram_b = lax.psum(local_b, 'ja')]
    pallas_call x0 -> x1, Pallas kernels: none -> 18.1 us  [local(): pl.pallas_call(functools.partial(kernel, n_ia, n_ja, n_ka, groups), out_s...]
    dot_general x5 -> x0, matrix products: 8.04 us -> none  [the longest x1 4.8 us: local(): jnp.einsum('rj,kji->rki', rank_b, tensor, preferred_element_type=jnp.floa...]
    unnamed x2 -> x1, local copies, waits for them, and re-layouts: 0.01 us -> 1.38 us
  transfers between devices with their start and end apart: 1 -> 0, of which waited for: 1 -> 0; matrix products, arithmetic and copies ran while one was open for 0% -> 0% of each run, Pallas kernels for 0% -> 0%
where the time goes in v1:
time: 19.7 us; the launch traced here: 19.5 us
  Pallas kernels  18.1 us (92%)
  local copies, waits for them, and re-layouts  1.38 us (7%)
    pallas_call x1, Pallas kernels, local(): pl.pallas_call(functools.partial(kernel, n_ia, n_ja, n_ka, groups), out_s...  18.1 us
    unnamed x1, local copies, waits for them, and re-layouts  1.38 us

profile of v1, /device:TPU:0, one launch (start us, length us, event | category | flops | bytes accessed | tf_op | source)
XLA Modules:
  0.0 19.5 jit_solution(2270200403267975318)
XLA Ops:
  0.0 18.1 %shard_map.46 = f32[4,8,256]{2,1,0:T(8,128)} custom-call(f32[16,256,256]{2,1,0:T(8,128)} %t_hbm.1, f32[32,256]{1,0:T(8,128)} %a_hbm.1, f32[16,256]{1,0:T(8,128)} %b_hbm.1, f32[16,16]{1,0:T(8,128)} %c_hbm.1), custom_call_target="tpu_custom_call" | custom-call | flops 402653184 | bytes 4194304 | tf_op jit(solution)/shard_map/pallas_call | solution.py:204
  18.1 1.4 %copy.6 = f32[32,256]{1,0:T(8,128)} copy(f32[32,256]{1,0:T(8,128)} %bitcast.1) | data formatting | bytes 65536

commit v2 on v1

--- a/solution.py
+++ b/solution.py
@@ -89,7 +89,8 @@
         copy.start()
         gathers.append(copy)
 
-    for g in range(groups):
+    early = groups // 2
+    for g in range(early):
         loads[g].wait()
 
         @pl.loop(g * step, (g + 1) * step)
@@ -122,15 +123,27 @@
 
     bh, bl = split(rank_b)
     lhs = jnp.concatenate([bh, bl], axis=0)
+
+    def planes_of(g, total):
+        for k in range(g * step, (g + 1) * step):
+            if g < early:
+                high, low = th[k], tl[k]
+            else:
+                high, low = split(t_v[k])
+            wide = dot(lhs, high)
+            inner = wide[:ranks] + (wide[ranks:] + dot(bh, low))
+            total = total + inner * rank_c[:, k : k + 1]
+        return total
+
     total = jnp.zeros((ranks, il), F32)
-    for k in range(planes):
-        wide = dot(lhs, th[k])
-        inner = wide[:ranks] + (wide[ranks:] + dot(bh, tl[k]))
-        total = total + inner * rank_c[:, k : k + 1]
+    for g in range(early):
+        total = planes_of(g, total)
     narrow = dot(lhs, bh, NT)
     gram_b = narrow[:ranks] + (narrow[ranks:] + dot(bh, bl, NT))
 
     own_a.wait()
+    for load in loads[early:]:
+        load.wait()
     for d in range(1, n_ka):
         q = lax.rem(ka + n_ka - d, n_ka)
         pltpu.make_async_remote_copy(
@@ -143,6 +156,8 @@
         gram_c = gram_c + gc[q]
     share = jnp.concatenate([a_v[q] for q in range(n_ka)], axis=0)
     total = total - dot3(gram_b * gram_c, share)
+    for g in range(early, groups):
+        total = planes_of(g, total)
 
     for kk in range(n_ka):
         for jj in range(n_ja):
@@ -198,18 +213,18 @@
     ranks = rb * n_ia
     rows = ra // n_ja
     n_red = n_ja * n_ka
-    groups = 4 if planes % 4 == 0 else 1
+    groups = 4
     wide_c = -(-planes // 128) * 128
     dma = pltpu.SemaphoreType.DMA
     out = pl.pallas_call(
         functools.partial(kernel, n_ia, n_ja, n_ka, groups),
-        out_shape=jax.ShapeDtypeStruct((n_ja, rows, il), F32),
+        out_shape=pltpu.VMEM((n_ja, rows, il), F32),
         in_specs=[pl.BlockSpec(memory_space=pl.ANY)] * 4,
         out_specs=pl.BlockSpec(memory_space=pltpu.VMEM),
         scratch_shapes=[
             pltpu.VMEM((planes, jl, il), F32),
-            pltpu.VMEM((planes, jl, il), BF16),
-            pltpu.VMEM((planes, jl, il), BF16),
+            pltpu.VMEM((planes // 2, jl, il), BF16),
+            pltpu.VMEM((planes // 2, jl, il), BF16),
             pltpu.VMEM((n_ia, rb, jl + wide_c), F32),
             pltpu.VMEM((rb, planes), F32),
             pltpu.VMEM((n_ka, ra, il), F32),

time: 19.7 us -> 18.5 us (0.939)
  local copies, waits for them, and re-layouts: 1.38 us -> 0.62 us
  Pallas kernels: 18.1 us -> 17.7 us
    unnamed x1, local copies, waits for them, and re-layouts: 1.38 us -> 0.62 us
    pallas_call x1, Pallas kernels: 18.1 us -> 17.7 us  [local(): pl.pallas_call(functools.partial(kernel, n_ia, n_ja, n_ka, groups), out_s...]
where the time goes in v2:
time: 18.5 us; the launch traced here: 18.3 us
  Pallas kernels  17.7 us (96%)
  local copies, waits for them, and re-layouts  0.62 us (3%)
    pallas_call x1, Pallas kernels, local(): pl.pallas_call(functools.partial(kernel, n_ia, n_ja, n_ka, groups), out_s...  17.7 us
    unnamed x1, local copies, waits for them, and re-layouts  0.62 us

profile of v2, /device:TPU:0, one launch (start us, length us, event | category | flops | bytes accessed | tf_op | source)
XLA Modules:
  0.0 18.3 jit_solution(5313040880291867718)
XLA Ops:
  0.0 17.7 %shard_map.46 = f32[4,8,256]{2,1,0:T(8,128)S(1)} custom-call(f32[16,256,256]{2,1,0:T(8,128)} %t_hbm.1, f32[32,256]{1,0:T(8,128)} %a_hbm.1, f32[16,256]{1,0:T(8,128)} %b_hbm.1, f32[16,16]{1,0:T(8,128)} %c_hbm.1), custom_call_target="tpu_custom_call" | custom-call | flops 402653184 | bytes 4194304 | tf_op jit(solution)/shard_map/pallas_call | solution.py:219
  17.7 0.6 %copy.6 = f32[32,256]{1,0:T(8,128)} copy(f32[32,256]{1,0:T(8,128)S(1)} %bitcast.1) | data formatting | bytes 65536

commit v3 on v2

--- a/solution.py
+++ b/solution.py
@@ -33,7 +33,7 @@
     n_ia, n_ja, n_ka, groups,
     t_hbm, a_hbm, b_hbm, c_hbm, out_ref,
     t_v, th, tl, pack, c_v, a_v, gc, part, recv,
-    t_sem, loc_sem, pack_send, pack_recv, gc_send, gc_recv,
+    t_sem, loc_sem, up_send, pack_send, pack_recv, gc_send, gc_recv,
     rs_send, rs_recv, ag_send, ag_recv,
 ):
     ia, ja, ka = lax.axis_index("ia"), lax.axis_index("ja"), lax.axis_index("ka")
@@ -46,6 +46,20 @@
     me = ja * n_ka + ka
     step = planes // groups
 
+    barrier = pltpu.get_barrier_semaphore()
+    for q in range(n_ia):
+
+        @pl.when((q > ia) | (q == ia - 1))
+        def _():
+            pl.semaphore_signal(barrier, inc=1, device_id={"ia": q}, device_id_type=MESH)
+
+    for d in range(1, n_red):
+        peer = lax.rem(me + d, n_red)
+        pl.semaphore_signal(
+            barrier, inc=1, device_id={"ja": peer // n_ka, "ka": lax.rem(peer, n_ka)},
+            device_id_type=MESH,
+        )
+
     own_b = pltpu.make_async_copy(b_hbm, pack.at[ia, :, pl.ds(0, jl)], loc_sem.at[0])
     own_c = pltpu.make_async_copy(c_hbm, c_v, loc_sem.at[1])
     own_b.start()
@@ -60,34 +74,45 @@
     a_v[...] = jnp.zeros_like(a_v)
     own_a = pltpu.make_async_copy(a_hbm, a_v.at[ka], loc_sem.at[2])
     own_a.start()
-
-    barrier = pltpu.get_barrier_semaphore()
-    for d in range(1, n_ia):
-        pl.semaphore_signal(
-            barrier, inc=1, device_id={"ia": lax.rem(ia + d, n_ia)}, device_id_type=MESH
-        )
-    for d in range(1, n_red):
-        peer = lax.rem(me + d, n_red)
-        pl.semaphore_signal(
-            barrier, inc=1, device_id={"ja": peer // n_ka, "ka": lax.rem(peer, n_ka)},
-            device_id_type=MESH,
-        )
     own_c.wait()
     pack[ia, :, jl:] = jnp.concatenate(
         [c_v[...], jnp.zeros((rb, pack.shape[2] - jl - planes), F32)], axis=1
     )
     own_b.wait()
-    pl.semaphore_wait(barrier, n_ia - 1 + n_red - 1)
-
-    gathers = []
-    for d in range(1, n_ia):
-        copy = pltpu.make_async_remote_copy(
-            src_ref=pack.at[ia], dst_ref=pack.at[ia],
-            send_sem=pack_send.at[d - 1], recv_sem=pack_recv.at[ia],
-            device_id={"ia": lax.rem(ia + d, n_ia)}, device_id_type=MESH,
-        )
-        copy.start()
-        gathers.append(copy)
+    pl.semaphore_wait(barrier, n_red - 1 + ia + jnp.where(ia < n_ia - 1, 1, 0))
+
+    def passed(slot, to, sem):
+        return pltpu.make_async_remote_copy(
+            src_ref=pack.at[slot], dst_ref=pack.at[slot],
+            send_sem=sem, recv_sem=pack_recv.at[slot],
+            device_id={"ia": to}, device_id_type=MESH,
+        )
+
+    def upward(slot):
+        return passed(slot, lax.rem(ia + 1, n_ia), up_send.at[slot])
+
+    def downward(to):
+        return passed(ia, to, pack_send.at[to])
+
+    @pl.when(ia < n_ia - 1)
+    def _():
+        upward(ia).start()
+
+    for q in range(n_ia - 1):
+
+        @pl.when(q < ia)
+        def _():
+            downward(q).start()
+
+    for q in reversed(range(n_ia - 1)):
+
+        @pl.when(q < ia)
+        def _():
+            passed(q, q, pack_send.at[q]).wait_recv()
+
+        @pl.when((q < ia) & (ia < n_ia - 1))
+        def _():
+            upward(q).start()
 
     early = groups // 2
     for g in range(early):
@@ -99,27 +124,15 @@
             th[k] = high
             tl[k] = low
 
-    for d in range(1, n_ia):
-        q = lax.rem(ia + n_ia - d, n_ia)
-        pltpu.make_async_remote_copy(
-            src_ref=pack.at[q], dst_ref=pack.at[q],
-            send_sem=pack_send.at[d - 1], recv_sem=pack_recv.at[q],
-            device_id={"ia": q}, device_id_type=MESH,
-        ).wait_recv()
+    for q in range(1, n_ia):
+
+        @pl.when(q > ia)
+        def _():
+            passed(q, q, pack_send.at[q]).wait_recv()
+
     both = jnp.concatenate([pack[q] for q in range(n_ia)], axis=0)
     rank_b = both[:, :jl]
     rank_c = both[:, jl:]
-
-    gc[ka] = dot3(rank_c, rank_c, NT)
-    grams = []
-    for d in range(1, n_ka):
-        copy = pltpu.make_async_remote_copy(
-            src_ref=gc.at[ka], dst_ref=gc.at[ka],
-            send_sem=gc_send.at[d - 1], recv_sem=gc_recv.at[ka],
-            device_id={"ka": lax.rem(ka + d, n_ka)}, device_id_type=MESH,
-        )
-        copy.start()
-        grams.append(copy)
 
     bh, bl = split(rank_b)
     lhs = jnp.concatenate([bh, bl], axis=0)
@@ -136,7 +149,20 @@
         return total
 
     total = jnp.zeros((ranks, il), F32)
-    for g in range(early):
+    total = planes_of(0, total)
+
+    gc[ka] = dot3(rank_c, rank_c, NT)
+    grams = []
+    for d in range(1, n_ka):
+        copy = pltpu.make_async_remote_copy(
+            src_ref=gc.at[ka], dst_ref=gc.at[ka],
+            send_sem=gc_send.at[d - 1], recv_sem=gc_recv.at[ka],
+            device_id={"ka": lax.rem(ka + d, n_ka)}, device_id_type=MESH,
+        )
+        copy.start()
+        grams.append(copy)
+
+    for g in range(1, early):
         total = planes_of(g, total)
     narrow = dot(lhs, bh, NT)
     gram_b = narrow[:ranks] + (narrow[ranks:] + dot(bh, bl, NT))
@@ -193,8 +219,18 @@
         )
         copy.start()
         spreads.append(copy)
-    for copy in gathers + grams + scatters:
+    for copy in grams + scatters:
         copy.wait_send()
+    for q in range(n_ia - 1):
+
+        @pl.when(q < ia)
+        def _():
+            downward(q).wait_send()
+
+        @pl.when((q <= ia) & (ia < n_ia - 1))
+        def _():
+            upward(q).wait_send()
+
     for d in range(1, n_ja):
         q = lax.rem(ja + n_ja - d, n_ja)
         pltpu.make_async_remote_copy(
@@ -235,6 +271,7 @@
             dma((3,)),
             dma((n_ia,)),
             dma((n_ia,)),
+            dma((n_ia,)),
             dma((n_ka,)),
             dma((n_ka,)),
             dma((n_red,)),

time: 18.5 us -> 18.6 us (level)
  no operation moved by 1% of the time
where the time goes in v3:
time: 18.6 us; the launch traced here: 18.4 us
  Pallas kernels  17.7 us (95%)
  local copies, waits for them, and re-layouts  0.62 us (3%)
    pallas_call x1, Pallas kernels, local(): pl.pallas_call(functools.partial(kernel, n_ia, n_ja, n_ka, groups), out_s...  17.7 us
    unnamed x1, local copies, waits for them, and re-layouts  0.62 us

profile of v3, /device:TPU:0, one launch (start us, length us, event | category | flops | bytes accessed | tf_op | source)
XLA Modules:
  0.0 18.4 jit_solution(2059187560127636031)
XLA Ops:
  0.0 17.7 %shard_map.46 = f32[4,8,256]{2,1,0:T(8,128)S(1)} custom-call(f32[16,256,256]{2,1,0:T(8,128)} %t_hbm.1, f32[32,256]{1,0:T(8,128)} %a_hbm.1, f32[16,256]{1,0:T(8,128)} %b_hbm.1, f32[16,16]{1,0:T(8,128)} %c_hbm.1), custom_call_target="tpu_custom_call" | custom-call | flops 402653184 | bytes 4194304 | tf_op jit(solution)/shard_map/pallas_call | solution.py:255
  17.8 0.6 %copy.6 = f32[32,256]{1,0:T(8,128)} copy(f32[32,256]{1,0:T(8,128)S(1)} %bitcast.1) | data formatting | bytes 65536

commit v4 on v1

--- a/solution.py
+++ b/solution.py
@@ -46,6 +46,17 @@
     me = ja * n_ka + ka
     step = planes // groups
 
+    barrier = pltpu.get_barrier_semaphore()
+    for d in range(1, n_ia):
+        pl.semaphore_signal(
+            barrier, inc=1, device_id={"ia": lax.rem(ia + d, n_ia)}, device_id_type=MESH
+        )
+    for d in range(1, n_red):
+        peer = lax.rem(me + d, n_red)
+        pl.semaphore_signal(
+            barrier, inc=1, device_id={"ja": peer // n_ka, "ka": lax.rem(peer, n_ka)},
+            device_id_type=MESH,
+        )
     own_b = pltpu.make_async_copy(b_hbm, pack.at[ia, :, pl.ds(0, jl)], loc_sem.at[0])
     own_c = pltpu.make_async_copy(c_hbm, c_v, loc_sem.at[1])
     own_b.start()
@@ -61,17 +72,6 @@
     own_a = pltpu.make_async_copy(a_hbm, a_v.at[ka], loc_sem.at[2])
     own_a.start()
 
-    barrier = pltpu.get_barrier_semaphore()
-    for d in range(1, n_ia):
-        pl.semaphore_signal(
-            barrier, inc=1, device_id={"ia": lax.rem(ia + d, n_ia)}, device_id_type=MESH
-        )
-    for d in range(1, n_red):
-        peer = lax.rem(me + d, n_red)
-        pl.semaphore_signal(
-            barrier, inc=1, device_id={"ja": peer // n_ka, "ka": lax.rem(peer, n_ka)},
-            device_id_type=MESH,
-        )
     own_c.wait()
     pack[ia, :, jl:] = jnp.concatenate(
         [c_v[...], jnp.zeros((rb, pack.shape[2] - jl - planes), F32)], axis=1
@@ -122,14 +122,21 @@
 
     bh, bl = split(rank_b)
     lhs = jnp.concatenate([bh, bl], axis=0)
-    total = jnp.zeros((ranks, il), F32)
-    for k in range(planes):
-        wide = dot(lhs, th[k])
-        inner = wide[:ranks] + (wide[ranks:] + dot(bh, tl[k]))
-        total = total + inner * rank_c[:, k : k + 1]
+    lane = lax.broadcasted_iota(jnp.int32, rank_c.shape, 1)
+
+    def planes_of(g, total):
+        for u in range(step):
+            k = g * step + u
+            column = jnp.sum(jnp.where(lane == k, rank_c, 0.0), axis=1, keepdims=True)
+            wide = dot(lhs, th[k])
+            inner = wide[:ranks] + (wide[ranks:] + dot(bh, tl[k]))
+            total = total + inner * column
+        return total
+
+    total = lax.fori_loop(0, groups - 1, planes_of, jnp.zeros((ranks, il), F32))
+
     narrow = dot(lhs, bh, NT)
     gram_b = narrow[:ranks] + (narrow[ranks:] + dot(bh, bl, NT))
-
     own_a.wait()
     for d in range(1, n_ka):
         q = lax.rem(ka + n_ka - d, n_ka)
@@ -143,6 +150,7 @@
         gram_c = gram_c + gc[q]
     share = jnp.concatenate([a_v[q] for q in range(n_ka)], axis=0)
     total = total - dot3(gram_b * gram_c, share)
+    total = planes_of(groups - 1, total)
 
     for kk in range(n_ka):
         for jj in range(n_ja):
@@ -198,12 +206,12 @@
     ranks = rb * n_ia
     rows = ra // n_ja
     n_red = n_ja * n_ka
-    groups = 4 if planes % 4 == 0 else 1
+    groups = 4
     wide_c = -(-planes // 128) * 128
     dma = pltpu.SemaphoreType.DMA
     out = pl.pallas_call(
         functools.partial(kernel, n_ia, n_ja, n_ka, groups),
-        out_shape=jax.ShapeDtypeStruct((n_ja, rows, il), F32),
+        out_shape=pltpu.VMEM((n_ja, rows, il), F32),
         in_specs=[pl.BlockSpec(memory_space=pl.ANY)] * 4,
         out_specs=pl.BlockSpec(memory_space=pltpu.VMEM),
         scratch_shapes=[

time: 19.7 us -> 18.6 us (0.944)
  local copies, waits for them, and re-layouts: 1.38 us -> 0.62 us
  Pallas kernels: 18.1 us -> 17.8 us
    unnamed x1, local copies, waits for them, and re-layouts: 1.38 us -> 0.62 us
    pallas_call x1, Pallas kernels: 18.1 us -> 17.8 us  [local(): pl.pallas_call(functools.partial(kernel, n_ia, n_ja, n_ka, groups), out_s...]
where the time goes in v4:
time: 18.6 us; the launch traced here: 18.4 us
  Pallas kernels  17.8 us (96%)
  local copies, waits for them, and re-layouts  0.62 us (3%)
    pallas_call x1, Pallas kernels, local(): pl.pallas_call(functools.partial(kernel, n_ia, n_ja, n_ka, groups), out_s...  17.8 us
    unnamed x1, local copies, waits for them, and re-layouts  0.62 us

profile of v4, /device:TPU:0, one launch (start us, length us, event | category | flops | bytes accessed | tf_op | source)
XLA Modules:
  0.0 18.4 jit_solution(102957934989831915)
XLA Ops:
  0.0 17.8 %shard_map.46 = f32[4,8,256]{2,1,0:T(8,128)S(1)} custom-call(f32[16,256,256]{2,1,0:T(8,128)} %t_hbm.1, f32[32,256]{1,0:T(8,128)} %a_hbm.1, f32[16,256]{1,0:T(8,128)} %b_hbm.1, f32[16,16]{1,0:T(8,128)} %c_hbm.1), custom_call_target="tpu_custom_call" | custom-call | flops 402653184 | bytes 4194304 | tf_op jit(solution)/shard_map/pallas_call | solution.py:212
  17.8 0.6 %copy.6 = f32[32,256]{1,0:T(8,128)} copy(f32[32,256]{1,0:T(8,128)S(1)} %bitcast.1) | data formatting | bytes 65536

commit v5 on v4

--- a/solution.py
+++ b/solution.py
@@ -51,7 +51,8 @@
         pl.semaphore_signal(
             barrier, inc=1, device_id={"ia": lax.rem(ia + d, n_ia)}, device_id_type=MESH
         )
-    for d in range(1, n_red):
+    @pl.loop(1, n_red)
+    def _(d):
         peer = lax.rem(me + d, n_red)
         pl.semaphore_signal(
             barrier, inc=1, device_id={"ja": peer // n_ka, "ka": lax.rem(peer, n_ka)},
@@ -95,8 +96,9 @@
         @pl.loop(g * step, (g + 1) * step)
         def _(k):
             high, low = split(t_v[k])
-            th[k] = high
-            tl[k] = low
+            columns = pl.ds(pl.multiple_of(k * il, il), il)
+            th[:, columns] = high
+            tl[:, columns] = low
 
     for d in range(1, n_ia):
         q = lax.rem(ia + n_ia - d, n_ia)
@@ -125,12 +127,14 @@
     lane = lax.broadcasted_iota(jnp.int32, rank_c.shape, 1)
 
     def planes_of(g, total):
+        columns = pl.ds(pl.multiple_of(g * (step * il), il), step * il)
+        wide = dot(lhs, th[:, columns])
+        inner = wide[:ranks] + (wide[ranks:] + dot(bh, tl[:, columns]))
         for u in range(step):
-            k = g * step + u
-            column = jnp.sum(jnp.where(lane == k, rank_c, 0.0), axis=1, keepdims=True)
-            wide = dot(lhs, th[k])
-            inner = wide[:ranks] + (wide[ranks:] + dot(bh, tl[k]))
-            total = total + inner * column
+            column = jnp.sum(
+                jnp.where(lane == g * step + u, rank_c, 0.0), axis=1, keepdims=True
+            )
+            total = total + inner[:, u * il : (u + 1) * il] * column
         return total
 
     total = lax.fori_loop(0, groups - 1, planes_of, jnp.zeros((ranks, il), F32))
@@ -156,25 +160,29 @@
         for jj in range(n_ja):
             low = kk * ra + jj * rows
             part[jj * n_ka + kk] = total[low : low + rows]
-    scatters = []
-    for d in range(1, n_red):
+
+    def scatter(d):
         peer = lax.rem(me + d, n_red)
-        copy = pltpu.make_async_remote_copy(
+        return pltpu.make_async_remote_copy(
             src_ref=part.at[peer], dst_ref=recv.at[me],
             send_sem=rs_send.at[d - 1], recv_sem=rs_recv.at[me],
             device_id={"ja": peer // n_ka, "ka": lax.rem(peer, n_ka)}, device_id_type=MESH,
         )
-        copy.start()
-        scatters.append(copy)
-    summed = part[me]
-    for d in range(1, n_red):
+
+    @pl.loop(1, n_red)
+    def _(d):
+        scatter(d).start()
+
+    def gather_sum(d, summed):
         q = lax.rem(me + n_red - d, n_red)
         pltpu.make_async_remote_copy(
             src_ref=part.at[q], dst_ref=recv.at[q],
             send_sem=rs_send.at[d - 1], recv_sem=rs_recv.at[q],
             device_id={"ja": q // n_ka, "ka": lax.rem(q, n_ka)}, device_id_type=MESH,
         ).wait_recv()
-        summed = summed + recv[q]
+        return summed + recv[q]
+
+    summed = lax.fori_loop(1, n_red, gather_sum, part[me])
 
     out_ref[ja] = summed
     spreads = []
@@ -186,8 +194,13 @@
         )
         copy.start()
         spreads.append(copy)
-    for copy in gathers + grams + scatters:
+    for copy in gathers + grams:
         copy.wait_send()
+
+    @pl.loop(1, n_red)
+    def _(d):
+        scatter(d).wait_send()
+
     for d in range(1, n_ja):
         q = lax.rem(ja + n_ja - d, n_ja)
         pltpu.make_async_remote_copy(
@@ -216,8 +229,8 @@
         out_specs=pl.BlockSpec(memory_space=pltpu.VMEM),
         scratch_shapes=[
             pltpu.VMEM((planes, jl, il), F32),
-            pltpu.VMEM((planes, jl, il), BF16),
-            pltpu.VMEM((planes, jl, il), BF16),
+            pltpu.VMEM((jl, planes * il), BF16),
+            pltpu.VMEM((jl, planes * il), BF16),
             pltpu.VMEM((n_ia, rb, jl + wide_c), F32),
             pltpu.VMEM((rb, planes), F32),
             pltpu.VMEM((n_ka, ra, il), F32),

time: 18.6 us -> 18.6 us (level)
  no operation moved by 1% of the time
where the time goes in v5:
time: 18.6 us; the launch traced here: 18.4 us
  Pallas kernels  17.8 us (96%)
  local copies, waits for them, and re-layouts  0.62 us (3%)
    pallas_call x1, Pallas kernels, local(): pl.pallas_call(functools.partial(kernel, n_ia, n_ja, n_ka, groups), out_s...  17.8 us
    unnamed x1, local copies, waits for them, and re-layouts  0.62 us

profile of v5, /device:TPU:0, one launch (start us, length us, event | category | flops | bytes accessed | tf_op | source)
XLA Modules:
  0.0 18.4 jit_solution(8485603037235968083)
XLA Ops:
  0.0 17.8 %shard_map.46 = f32[4,8,256]{2,1,0:T(8,128)S(1)} custom-call(f32[16,256,256]{2,1,0:T(8,128)} %t_hbm.1, f32[32,256]{1,0:T(8,128)} %a_hbm.1, f32[16,256]{1,0:T(8,128)} %b_hbm.1, f32[16,16]{1,0:T(8,128)} %c_hbm.1), custom_call_target="tpu_custom_call" | custom-call | flops 402653184 | bytes 4194304 | tf_op jit(solution)/shard_map/pallas_call | solution.py:225
  17.8 0.6 %copy.6 = f32[32,256]{1,0:T(8,128)} copy(f32[32,256]{1,0:T(8,128)S(1)} %bitcast.1) | data formatting | bytes 65536

commit v6 on v5

v6 whole, which is shorter than its diff:
```python
import functools

import jax
import jax.numpy as jnp
from jax import lax
from jax.experimental import pallas as pl
from jax.experimental.pallas import tpu as pltpu
from jax.sharding import PartitionSpec as P

MESH = pl.DeviceIdType.MESH
F32 = jnp.float32
BF16 = jnp.bfloat16
NN = (((1,), (0,)), ((), ()))
NT = (((1,), (1,)), ((), ()))


def split(x):
    high = x.astype(BF16)
    return high, (x - high.astype(F32)).astype(BF16)


def dot(x, y, dims=NN):
    return lax.dot_general(x, y, dims, preferred_element_type=F32)


def dot3(x, y, dims=NN):
    xh, xl = split(x)
    yh, yl = split(y)
    return dot(xh, yh, dims) + (dot(xh, yl, dims) + dot(xl, yh, dims))


def kernel(
    n_ia, n_ja, n_ka, groups,
    t_hbm, a_hbm, b_hbm, c_hbm, out_ref,
    t_v, th, tl, pack, c_v, a_v, gc, part, recv,
    t_sem, loc_sem, pack_send, pack_recv, gc_send, gc_recv,
    red_send, red_recv,
):
    ia, ja, ka = lax.axis_index("ia"), lax.axis_index("ja"), lax.axis_index("ka")
    planes, jl, il = t_v.shape
    rb = pack.shape[1]
    ranks = rb * n_ia
    ra = a_v.shape[1]
    halves, hw = part.shape[0], part.shape[3]
    n_red = n_ja * n_ka
    me = ja * n_ka + ka
    step = planes // groups

    barrier = pltpu.get_barrier_semaphore()
    for d in range(1, n_ia):
        pl.semaphore_signal(
            barrier, inc=1, device_id={"ia": lax.rem(ia + d, n_ia)}, device_id_type=MESH
        )
    @pl.loop(1, n_red)
    def _(d):
        peer = lax.rem(me + d, n_red)
        pl.semaphore_signal(
            barrier, inc=1, device_id={"ja": peer // n_ka, "ka": lax.rem(peer, n_ka)},
            device_id_type=MESH,
        )
    own_b = pltpu.make_async_copy(b_hbm, pack.at[ia, :, pl.ds(0, jl)], loc_sem.at[0])
    own_c = pltpu.make_async_copy(c_hbm, c_v, loc_sem.at[1])
    own_b.start()
    own_c.start()
    loads = []
    for g in range(groups):
        load = pltpu.make_async_copy(
            t_hbm.at[pl.ds(g * step, step)], t_v.at[pl.ds(g * step, step)], t_sem.at[g]
        )
        load.start()
        loads.append(load)
    a_v[...] = jnp.zeros_like(a_v)
    own_a = pltpu.make_async_copy(a_hbm, a_v.at[ka], loc_sem.at[2])
    own_a.start()

    own_c.wait()
    pack[ia, :, jl:] = jnp.concatenate(
        [c_v[...], jnp.zeros((rb, pack.shape[2] - jl - planes), F32)], axis=1
    )
    own_b.wait()
    pl.semaphore_wait(barrier, n_ia - 1 + n_red - 1)

    gathers = []
    for d in range(1, n_ia):
        copy = pltpu.make_async_remote_copy(
            src_ref=pack.at[ia], dst_ref=pack.at[ia],
            send_sem=pack_send.at[d - 1], recv_sem=pack_recv.at[ia],
            device_id={"ia": lax.rem(ia + d, n_ia)}, device_id_type=MESH,
        )
        copy.start()
        gathers.append(copy)

    for g in range(groups):
        loads[g].wait()

        @pl.loop(g * step, (g + 1) * step)
        def _(k):
            high, low = split(t_v[k])
            columns = pl.ds(pl.multiple_of(k * hw, hw), hw)
            for h in range(halves):
                th[h, :, columns] = high[:, h * hw : (h + 1) * hw]
                tl[h, :, columns] = low[:, h * hw : (h + 1) * hw]

    for d in range(1, n_ia):
        q = lax.rem(ia + n_ia - d, n_ia)
        pltpu.make_async_remote_copy(
            src_ref=pack.at[q], dst_ref=pack.at[q],
            send_sem=pack_send.at[d - 1], recv_sem=pack_recv.at[q],
            device_id={"ia": q}, device_id_type=MESH,
        ).wait_recv()
    both = jnp.concatenate([pack[q] for q in range(n_ia)], axis=0)
    rank_b = both[:, :jl]
    rank_c = both[:, jl:]

    gc[ka] = dot3(rank_c, rank_c, NT)
    grams = []
    for d in range(1, n_ka):
        copy = pltpu.make_async_remote_copy(
            src_ref=gc.at[ka], dst_ref=gc.at[ka],
            send_sem=gc_send.at[d - 1], recv_sem=gc_recv.at[ka],
            device_id={"ka": lax.rem(ka + d, n_ka)}, device_id_type=MESH,
        )
        copy.start()
        grams.append(copy)

    bh, bl = split(rank_b)
    lhs = jnp.concatenate([bh, bl], axis=0)
    lane = lax.broadcasted_iota(jnp.int32, rank_c.shape, 1)

    narrow = dot(lhs, bh, NT)
    gram_b = narrow[:ranks] + (narrow[ranks:] + dot(bh, bl, NT))

    def exchange(h, d):
        peer = lax.rem(me + d, n_red)
        return pltpu.make_async_remote_copy(
            src_ref=part.at[h, lax.rem(peer, n_ka)], dst_ref=recv.at[h, me],
            send_sem=red_send.at[h, d - 1], recv_sem=red_recv.at[h, me],
            device_id={"ja": peer // n_ka, "ka": lax.rem(peer, n_ka)}, device_id_type=MESH,
        )

    for h in range(halves):

        def planes_of(g, total):
            columns = pl.ds(pl.multiple_of(g * (step * hw), step * hw), step * hw)
            wide = dot(lhs, th[h, :, columns])
            inner = wide[:ranks] + (wide[ranks:] + dot(bh, tl[h, :, columns]))
            for u in range(step):
                column = jnp.sum(
                    jnp.where(lane == g * step + u, rank_c, 0.0), axis=1, keepdims=True
                )
                total = total + inner[:, u * hw : (u + 1) * hw] * column
            return total

        total = lax.fori_loop(0, groups, planes_of, jnp.zeros((ranks, hw), F32))

        if h == 0:
            own_a.wait()
            for d in range(1, n_ka):
                q = lax.rem(ka + n_ka - d, n_ka)
                pltpu.make_async_remote_copy(
                    src_ref=gc.at[q], dst_ref=gc.at[q],
                    send_sem=gc_send.at[d - 1], recv_sem=gc_recv.at[q],
                    device_id={"ka": q}, device_id_type=MESH,
                ).wait_recv()
            gram_c = gc[0]
            for q in range(1, n_ka):
                gram_c = gram_c + gc[q]
            share = jnp.concatenate([a_v[q] for q in range(n_ka)], axis=0)
            correction = dot3(gram_b * gram_c, share)
        total = total - correction[:, h * hw : (h + 1) * hw]

        for kk in range(n_ka):
            part[h, kk] = total[kk * ra : (kk + 1) * ra]

        @pl.loop(1, n_red)
        def _(d):
            exchange(h, d).start()

        recv[h, me] = part[h, ka]

    for copy in gathers + grams:
        copy.wait_send()

    for h in range(halves):

        @pl.loop(1, n_red)
        def _(d):
            q = lax.rem(me + n_red - d, n_red)
            pltpu.make_async_remote_copy(
                src_ref=part.at[h, ka], dst_ref=recv.at[h, q],
                send_sem=red_send.at[h, d - 1], recv_sem=red_recv.at[h, q],
                device_id={"ja": q // n_ka, "ka": lax.rem(q, n_ka)}, device_id_type=MESH,
            ).wait_recv()

        summed = recv[h, 0]
        for q in range(1, n_red):
            summed = summed + recv[h, q]
        out_ref[:, h * hw : (h + 1) * hw] = summed

    for h in range(halves):

        @pl.loop(1, n_red)
        def _(d):
            exchange(h, d).wait_send()


def local(sizes, tensor, factor_a, factor_b, factor_c):
    n_ia, n_ja, n_ka = sizes
    planes, jl, il = tensor.shape
    ra, rb = factor_a.shape[0], factor_b.shape[0]
    ranks = rb * n_ia
    halves = 2
    hw = il // halves
    n_red = n_ja * n_ka
    groups = 4
    wide_c = -(-planes // 128) * 128
    dma = pltpu.SemaphoreType.DMA
    return pl.pallas_call(
        functools.partial(kernel, n_ia, n_ja, n_ka, groups),
        out_shape=pltpu.VMEM((ra, il), F32),
        in_specs=[pl.BlockSpec(memory_space=pl.ANY)] * 4,
        out_specs=pl.BlockSpec(memory_space=pltpu.VMEM),
        scratch_shapes=[
            pltpu.VMEM((planes, jl, il), F32),
            pltpu.VMEM((halves, jl, planes * hw), BF16),
            pltpu.VMEM((halves, jl, planes * hw), BF16),
            pltpu.VMEM((n_ia, rb, jl + wide_c), F32),
            pltpu.VMEM((rb, planes), F32),
            pltpu.VMEM((n_ka, ra, il), F32),
            pltpu.VMEM((n_ka, ranks, ranks), F32),
            pltpu.VMEM((halves, n_ka, ra, hw), F32),
            pltpu.VMEM((halves, n_red, ra, hw), F32),
            dma((groups,)),
            dma((3,)),
            dma((n_ia,)),
            dma((n_ia,)),
            dma((n_ka,)),
            dma((n_ka,)),
            dma((halves, n_red)),
            dma((halves, n_red)),
        ],
        compiler_params=pltpu.CompilerParams(
            collective_id=0, has_side_effects=True, vmem_limit_bytes=56 * 2**20
        ),
        cost_estimate=pl.CostEstimate(
            flops=6 * ranks * planes * jl * il,
            bytes_accessed=4 * planes * jl * il,
            transcendentals=0,
        ),
    )(tensor, factor_a, factor_b, factor_c)


def solution(mesh):
    sizes = tuple(mesh.shape[name] for name in ("ia", "ja", "ka"))
    in_specs = (P("ka", "ja", "ia"), P("ka", "ia"), P("ia", "ja"), P("ia", "ka"))
    return jax.shard_map(
        functools.partial(local, sizes), mesh=mesh, in_specs=in_specs,
        out_specs=P("ka", "ia"), check_vma=False,
    )
```

time: 18.6 us -> 16.5 us (0.89)
  Pallas kernels: 17.8 us -> 15.8 us
    pallas_call x1, Pallas kernels: 17.8 us -> 15.8 us  [local(): pl.pallas_call(functools.partial(kernel, n_ia, n_ja, n_ka, groups), out_s...]
where the time goes in v6:
time: 16.5 us; the launch traced here: 16.4 us
  Pallas kernels  15.8 us (96%)
  local copies, waits for them, and re-layouts  0.62 us (4%)
    pallas_call x1, Pallas kernels, local(): pl.pallas_call(functools.partial(kernel, n_ia, n_ja, n_ka, groups), out_s...  15.8 us
    unnamed x1, local copies, waits for them, and re-layouts  0.62 us

profile of v6, /device:TPU:0, one launch (start us, length us, event | category | flops | bytes accessed | tf_op | source)
XLA Modules:
  0.0 16.4 jit_solution(10293299101033948170)
XLA Ops:
  0.0 15.8 %shard_map.46 = f32[32,256]{1,0:T(8,128)S(1)} custom-call(f32[16,256,256]{2,1,0:T(8,128)} %t_hbm.1, f32[32,256]{1,0:T(8,128)} %a_hbm.1, f32[16,256]{1,0:T(8,128)} %b_hbm.1, f32[16,16]{1,0:T(8,128)} %c_hbm.1), custom_call_target="tpu_custom_call" | custom-call | flops 402653184 | bytes 4194304 | tf_op jit(solution)/shard_map/pallas_call | solution.py:218
  15.8 0.6 %copy.6 = f32[32,256]{1,0:T(8,128)} copy(f32[32,256]{1,0:T(8,128)S(1)} %shard_map.46) | data formatting | bytes 65536

commit v7 on v6

v7 whole, which is shorter than its diff:
```python
import functools

import jax
import jax.numpy as jnp
from jax import lax
from jax.experimental import pallas as pl
from jax.experimental.pallas import tpu as pltpu
from jax.sharding import PartitionSpec as P

MESH = pl.DeviceIdType.MESH
F32 = jnp.float32
BF16 = jnp.bfloat16
NN = (((1,), (0,)), ((), ()))
NT = (((1,), (1,)), ((), ()))


def split(x):
    high = x.astype(BF16)
    return high, (x - high.astype(F32)).astype(BF16)


def dot(x, y, dims=NN):
    return lax.dot_general(x, y, dims, preferred_element_type=F32)


def dot3(x, y, dims=NN):
    xh, xl = split(x)
    yh, yl = split(y)
    return dot(xh, yh, dims) + (dot(xh, yl, dims) + dot(xl, yh, dims))


def kernel(
    n_ia, n_ja, n_ka, groups,
    t_hbm, a_hbm, b_hbm, c_hbm, out_ref,
    t_v, th, tl, b_all, c_all, a_all, part, recv,
    t_sem, loc_sem, fac_send, fac_recv, a_send, a_recv,
    red_send, red_recv,
):
    ia, ja, ka = lax.axis_index("ia"), lax.axis_index("ja"), lax.axis_index("ka")
    planes, jl, il = t_v.shape
    ranks = b_all.shape[1] * n_ia
    ra = a_all.shape[1]
    halves, hw = part.shape[0], part.shape[3]
    n_red = n_ja * n_ka
    me = ja * n_ka + ka
    step = planes // groups

    barrier = pltpu.get_barrier_semaphore()
    for d in range(1, n_ia):
        pl.semaphore_signal(
            barrier, inc=1, device_id={"ia": lax.rem(ia + d, n_ia)}, device_id_type=MESH
        )
    @pl.loop(1, n_red)
    def _(d):
        peer = lax.rem(me + d, n_red)
        pl.semaphore_signal(
            barrier, inc=1, device_id={"ja": peer // n_ka, "ka": lax.rem(peer, n_ka)},
            device_id_type=MESH,
        )
    own = [
        pltpu.make_async_copy(b_hbm, b_all.at[ia], loc_sem.at[0]),
        pltpu.make_async_copy(c_hbm, c_all.at[ia], loc_sem.at[1]),
        pltpu.make_async_copy(a_hbm, a_all.at[ka], loc_sem.at[2]),
    ]
    loads = [
        pltpu.make_async_copy(
            t_hbm.at[pl.ds(g * step, step)], t_v.at[pl.ds(g * step, step)], t_sem.at[g]
        )
        for g in range(groups)
    ]
    for load in own + loads:
        load.start()
    pl.semaphore_wait(barrier, n_ia - 1 + n_red - 1)

    def factors(to, source, sem):
        return [
            pltpu.make_async_remote_copy(
                src_ref=src, dst_ref=dst.at[source],
                send_sem=fac_send.at[i, sem], recv_sem=fac_recv.at[i, source],
                device_id={"ia": to}, device_id_type=MESH,
            )
            for i, (src, dst) in enumerate(((b_hbm, b_all), (c_hbm, c_all)))
        ]

    def ranks_a(to, source, sem):
        return pltpu.make_async_remote_copy(
            src_ref=a_hbm, dst_ref=a_all.at[source],
            send_sem=a_send.at[sem], recv_sem=a_recv.at[source],
            device_id={"ka": to}, device_id_type=MESH,
        )

    sent = []
    for d in range(1, n_ia):
        sent += factors(lax.rem(ia + d, n_ia), ia, d - 1)
    for d in range(1, n_ka):
        sent.append(ranks_a(lax.rem(ka + d, n_ka), ka, d - 1))
    for copy in sent:
        copy.start()

    for g in range(groups):
        loads[g].wait()

        @pl.loop(g * step, (g + 1) * step)
        def _(k):
            high, low = split(t_v[k])
            columns = pl.ds(pl.multiple_of(k * hw, hw), hw)
            for h in range(halves):
                th[h, :, columns] = high[:, h * hw : (h + 1) * hw]
                tl[h, :, columns] = low[:, h * hw : (h + 1) * hw]

    for copy in own:
        copy.wait()
    for d in range(1, n_ka):
        q = lax.rem(ka + n_ka - d, n_ka)
        ranks_a(q, q, d - 1).wait_recv()
    for d in range(1, n_ia):
        q = lax.rem(ia + n_ia - d, n_ia)
        for copy in factors(q, q, d - 1):
            copy.wait_recv()
    rank_b = jnp.concatenate([b_all[q] for q in range(n_ia)], axis=0)
    rank_c = jnp.concatenate([c_all[q] for q in range(n_ia)], axis=0)
    share = jnp.concatenate([a_all[q] for q in range(n_ka)], axis=0)

    bh, bl = split(rank_b)
    lhs = jnp.concatenate([bh, bl], axis=0)
    def exchange(h, d):
        peer = lax.rem(me + d, n_red)
        return pltpu.make_async_remote_copy(
            src_ref=part.at[h, lax.rem(peer, n_ka)], dst_ref=recv.at[h, me],
            send_sem=red_send.at[h, d - 1], recv_sem=red_recv.at[h, me],
            device_id={"ja": peer // n_ka, "ka": lax.rem(peer, n_ka)}, device_id_type=MESH,
        )

    for h in range(halves):

        total = jnp.zeros((ranks, hw), F32)
        for g in range(groups):
            columns = pl.ds(g * step * hw, step * hw)
            wide = dot(lhs, th[h, :, columns])
            inner = wide[:ranks] + (wide[ranks:] + dot(bh, tl[h, :, columns]))
            for u in range(step):
                k = g * step + u
                total = total + inner[:, u * hw : (u + 1) * hw] * rank_c[:, k : k + 1]

            if h == 0 and g == 0:
                narrow = dot(lhs, bh, NT)
                gram_b = narrow[:ranks] + (narrow[ranks:] + dot(bh, bl, NT))
                gram_c = dot3(rank_c, rank_c, NT)
                correction = dot3(gram_b * gram_c, share)
        total = total - correction[:, h * hw : (h + 1) * hw]

        for kk in range(n_ka):
            part[h, kk] = total[kk * ra : (kk + 1) * ra]

        @pl.loop(1, n_red)
        def _(d):
            exchange(h, d).start()

        recv[h, me] = part[h, ka]

    for copy in sent:
        copy.wait_send()

    for h in range(halves):

        @pl.loop(1, n_red)
        def _(d):
            q = lax.rem(me + n_red - d, n_red)
            pltpu.make_async_remote_copy(
                src_ref=part.at[h, ka], dst_ref=recv.at[h, q],
                send_sem=red_send.at[h, d - 1], recv_sem=red_recv.at[h, q],
                device_id={"ja": q // n_ka, "ka": lax.rem(q, n_ka)}, device_id_type=MESH,
            ).wait_recv()

        summed = recv[h, 0]
        for q in range(1, n_red):
            summed = summed + recv[h, q]
        out_ref[:, h * hw : (h + 1) * hw] = summed

    for h in range(halves):

        @pl.loop(1, n_red)
        def _(d):
            exchange(h, d).wait_send()


def local(sizes, tensor, factor_a, factor_b, factor_c):
    n_ia, n_ja, n_ka = sizes
    planes, jl, il = tensor.shape
    ra, rb = factor_a.shape[0], factor_b.shape[0]
    ranks = rb * n_ia
    halves = 2
    hw = il // halves
    n_red = n_ja * n_ka
    groups = 4
    dma = pltpu.SemaphoreType.DMA
    return pl.pallas_call(
        functools.partial(kernel, n_ia, n_ja, n_ka, groups),
        out_shape=pltpu.VMEM((ra, il), F32),
        in_specs=[pl.BlockSpec(memory_space=pl.ANY)] * 4,
        out_specs=pl.BlockSpec(memory_space=pltpu.VMEM),
        scratch_shapes=[
            pltpu.VMEM((planes, jl, il), F32),
            pltpu.VMEM((halves, jl, planes * hw), BF16),
            pltpu.VMEM((halves, jl, planes * hw), BF16),
            pltpu.VMEM((n_ia, rb, jl), F32),
            pltpu.VMEM((n_ia, rb, planes), F32),
            pltpu.VMEM((n_ka, ra, il), F32),
            pltpu.VMEM((halves, n_ka, ra, hw), F32),
            pltpu.VMEM((halves, n_red, ra, hw), F32),
            dma((groups,)),
            dma((3,)),
            dma((2, n_ia)),
            dma((2, n_ia)),
            dma((n_ka,)),
            dma((n_ka,)),
            dma((halves, n_red)),
            dma((halves, n_red)),
        ],
        compiler_params=pltpu.CompilerParams(
            collective_id=0, has_side_effects=True, vmem_limit_bytes=56 * 2**20
        ),
        cost_estimate=pl.CostEstimate(
            flops=6 * ranks * planes * jl * il,
            bytes_accessed=4 * planes * jl * il,
            transcendentals=0,
        ),
    )(tensor, factor_a, factor_b, factor_c)


def solution(mesh):
    sizes = tuple(mesh.shape[name] for name in ("ia", "ja", "ka"))
    in_specs = (P("ka", "ja", "ia"), P("ka", "ia"), P("ia", "ja"), P("ia", "ka"))
    return jax.shard_map(
        functools.partial(local, sizes), mesh=mesh, in_specs=in_specs,
        out_specs=P("ka", "ia"), check_vma=False,
    )
```

time: 16.5 us -> 15.1 us (0.915)
  Pallas kernels: 15.8 us -> 14.3 us
    pallas_call x1, Pallas kernels: 15.8 us -> 14.3 us  [local(): pl.pallas_call(functools.partial(kernel, n_ia, n_ja, n_ka, groups), out_s...]
where the time goes in v7:
time: 15.1 us; the launch traced here: 15 us
  Pallas kernels  14.3 us (95%)
  local copies, waits for them, and re-layouts  0.62 us (4%)
    pallas_call x1, Pallas kernels, local(): pl.pallas_call(functools.partial(kernel, n_ia, n_ja, n_ka, groups), out_s...  14.3 us
    unnamed x1, local copies, waits for them, and re-layouts  0.62 us

profile of v7, /device:TPU:0, one launch (start us, length us, event | category | flops | bytes accessed | tf_op | source)
XLA Modules:
  0.0 15.0 jit_solution(15782110272791266961)
XLA Ops:
  0.0 14.3 %shard_map.46 = f32[32,256]{1,0:T(8,128)S(1)} custom-call(f32[16,256,256]{2,1,0:T(8,128)} %t_hbm.1, f32[32,256]{1,0:T(8,128)} %a_hbm.1, f32[16,256]{1,0:T(8,128)} %b_hbm.1, f32[16,16]{1,0:T(8,128)} %c_hbm.1), custom_call_target="tpu_custom_call" | custom-call | flops 402653184 | bytes 4194304 | tf_op jit(solution)/shard_map/pallas_call | solution.py:197
  14.3 0.6 %copy.6 = f32[32,256]{1,0:T(8,128)} copy(f32[32,256]{1,0:T(8,128)S(1)} %shard_map.46) | data formatting | bytes 65536

commit v8 on v7

--- a/solution.py
+++ b/solution.py
@@ -32,7 +32,7 @@
 def kernel(
     n_ia, n_ja, n_ka, groups,
     t_hbm, a_hbm, b_hbm, c_hbm, out_ref,
-    t_v, th, tl, b_all, c_all, a_all, part, recv,
+    t_v, th, b_all, c_all, a_all, part, recv,
     t_sem, loc_sem, fac_send, fac_recv, a_send, a_recv,
     red_send, red_recv,
 ):
@@ -102,11 +102,11 @@
 
         @pl.loop(g * step, (g + 1) * step)
         def _(k):
-            high, low = split(t_v[k])
-            columns = pl.ds(pl.multiple_of(k * hw, hw), hw)
+            high, low = split(t_v[k].T)
+            place = pl.ds(pl.multiple_of(k * hw, hw), hw)
             for h in range(halves):
-                th[h, :, columns] = high[:, h * hw : (h + 1) * hw]
-                tl[h, :, columns] = low[:, h * hw : (h + 1) * hw]
+                th[h, place, :jl] = high[h * hw : (h + 1) * hw]
+                th[h, place, jl:] = low[h * hw : (h + 1) * hw]
 
     for copy in own:
         copy.wait()
@@ -123,6 +123,14 @@
 
     bh, bl = split(rank_b)
     lhs = jnp.concatenate([bh, bl], axis=0)
+    stands = jnp.concatenate(
+        [lhs, jnp.concatenate([bh, jnp.zeros_like(bl)], axis=0)], axis=1
+    )
+    twice = jnp.concatenate([rank_c, rank_c], axis=0)
+    twice = jnp.concatenate(
+        [twice, jnp.zeros((2 * ranks, 128 - planes), F32)], axis=1
+    ).T
+
     def exchange(h, d):
         peer = lax.rem(me + d, n_red)
         return pltpu.make_async_remote_copy(
@@ -133,21 +141,20 @@
 
     for h in range(halves):
 
-        total = jnp.zeros((ranks, hw), F32)
+        flipped = jnp.zeros((hw, 2 * ranks), F32)
         for g in range(groups):
-            columns = pl.ds(g * step * hw, step * hw)
-            wide = dot(lhs, th[h, :, columns])
-            inner = wide[:ranks] + (wide[ranks:] + dot(bh, tl[h, :, columns]))
+            wide = dot(th[h, pl.ds(g * step * hw, step * hw), :], stands, NT)
             for u in range(step):
                 k = g * step + u
-                total = total + inner[:, u * hw : (u + 1) * hw] * rank_c[:, k : k + 1]
+                flipped = flipped + wide[u * hw : (u + 1) * hw] * twice[k : k + 1]
 
             if h == 0 and g == 0:
                 narrow = dot(lhs, bh, NT)
                 gram_b = narrow[:ranks] + (narrow[ranks:] + dot(bh, bl, NT))
                 gram_c = dot3(rank_c, rank_c, NT)
                 correction = dot3(gram_b * gram_c, share)
-        total = total - correction[:, h * hw : (h + 1) * hw]
+        total = flipped.T
+        total = total[:ranks] + total[ranks:] - correction[:, h * hw : (h + 1) * hw]
 
         for kk in range(n_ka):
             part[h, kk] = total[kk * ra : (kk + 1) * ra]
@@ -201,8 +208,7 @@
         out_specs=pl.BlockSpec(memory_space=pltpu.VMEM),
         scratch_shapes=[
             pltpu.VMEM((planes, jl, il), F32),
-            pltpu.VMEM((halves, jl, planes * hw), BF16),
-            pltpu.VMEM((halves, jl, planes * hw), BF16),
+            pltpu.VMEM((halves, planes * hw, 2 * jl), BF16),
             pltpu.VMEM((n_ia, rb, jl), F32),
             pltpu.VMEM((n_ia, rb, planes), F32),
             pltpu.VMEM((n_ka, ra, il), F32),

time: 15.1 us -> 15.7 us (1.040)
  Pallas kernels: 14.3 us -> 14.9 us
    pallas_call x1, Pallas kernels: 14.3 us -> 14.9 us  [local(): pl.pallas_call(functools.partial(kernel, n_ia, n_ja, n_ka, groups), out_s...]
where the time goes in v8:
time: 15.7 us; the launch traced here: 15.5 us
  Pallas kernels  14.9 us (95%)
  local copies, waits for them, and re-layouts  0.62 us (4%)
    pallas_call x1, Pallas kernels, local(): pl.pallas_call(functools.partial(kernel, n_ia, n_ja, n_ka, groups), out_s...  14.9 us
    unnamed x1, local copies, waits for them, and re-layouts  0.62 us

profile of v8, /device:TPU:0, one launch (start us, length us, event | category | flops | bytes accessed | tf_op | source)
XLA Modules:
  0.0 15.5 jit_solution(13627112673079879267)
XLA Ops:
  0.0 14.9 %shard_map.46 = f32[32,256]{1,0:T(8,128)S(1)} custom-call(f32[16,256,256]{2,1,0:T(8,128)} %t_hbm.1, f32[32,256]{1,0:T(8,128)} %a_hbm.1, f32[16,256]{1,0:T(8,128)} %b_hbm.1, f32[16,16]{1,0:T(8,128)} %c_hbm.1), custom_call_target="tpu_custom_call" | custom-call | flops 402653184 | bytes 4194304 | tf_op jit(solution)/shard_map/pallas_call | solution.py:204
  14.9 0.6 %copy.6 = f32[32,256]{1,0:T(8,128)} copy(f32[32,256]{1,0:T(8,128)S(1)} %shard_map.46) | data formatting | bytes 65536

commit v9 on v7

--- a/solution.py
+++ b/solution.py
@@ -102,11 +102,10 @@
 
         @pl.loop(g * step, (g + 1) * step)
         def _(k):
-            high, low = split(t_v[k])
+            high, low = split(t_v[k, :, :hw])
             columns = pl.ds(pl.multiple_of(k * hw, hw), hw)
-            for h in range(halves):
-                th[h, :, columns] = high[:, h * hw : (h + 1) * hw]
-                tl[h, :, columns] = low[:, h * hw : (h + 1) * hw]
+            th[:, columns] = high
+            tl[:, columns] = low
 
     for copy in own:
         copy.wait()
@@ -136,8 +135,20 @@
         total = jnp.zeros((ranks, hw), F32)
         for g in range(groups):
             columns = pl.ds(g * step * hw, step * hw)
-            wide = dot(lhs, th[h, :, columns])
-            inner = wide[:ranks] + (wide[ranks:] + dot(bh, tl[h, :, columns]))
+            if h == 0:
+                high, low = th[:, columns], tl[:, columns]
+            else:
+                high, low = split(
+                    jnp.concatenate(
+                        [
+                            t_v[k, :, h * hw : (h + 1) * hw]
+                            for k in range(g * step, (g + 1) * step)
+                        ],
+                        axis=1,
+                    )
+                )
+            wide = dot(lhs, high)
+            inner = wide[:ranks] + (wide[ranks:] + dot(bh, low))
             for u in range(step):
                 k = g * step + u
                 total = total + inner[:, u * hw : (u + 1) * hw] * rank_c[:, k : k + 1]
@@ -165,6 +176,7 @@
 
         @pl.loop(1, n_red)
         def _(d):
+            exchange(h, d).wait_send()
             q = lax.rem(me + n_red - d, n_red)
             pltpu.make_async_remote_copy(
                 src_ref=part.at[h, ka], dst_ref=recv.at[h, q],
@@ -176,12 +188,6 @@
         for q in range(1, n_red):
             summed = summed + recv[h, q]
         out_ref[:, h * hw : (h + 1) * hw] = summed
-
-    for h in range(halves):
-
-        @pl.loop(1, n_red)
-        def _(d):
-            exchange(h, d).wait_send()
 
 
 def local(sizes, tensor, factor_a, factor_b, factor_c):
@@ -201,8 +207,8 @@
         out_specs=pl.BlockSpec(memory_space=pltpu.VMEM),
         scratch_shapes=[
             pltpu.VMEM((planes, jl, il), F32),
-            pltpu.VMEM((halves, jl, planes * hw), BF16),
-            pltpu.VMEM((halves, jl, planes * hw), BF16),
+            pltpu.VMEM((jl, planes * hw), BF16),
+            pltpu.VMEM((jl, planes * hw), BF16),
             pltpu.VMEM((n_ia, rb, jl), F32),
             pltpu.VMEM((n_ia, rb, planes), F32),
             pltpu.VMEM((n_ka, ra, il), F32),

time: 15.1 us -> 15 us (level)
  no operation moved by 1% of the time
where the time goes in v9:
time: 15 us; the launch traced here: 14.9 us
  Pallas kernels  14.2 us (95%)
  local copies, waits for them, and re-layouts  0.62 us (4%)
    pallas_call x1, Pallas kernels, local(): pl.pallas_call(functools.partial(kernel, n_ia, n_ja, n_ka, groups), out_s...  14.2 us
    unnamed x1, local copies, waits for them, and re-layouts  0.62 us

profile of v9, /device:TPU:0, one launch (start us, length us, event | category | flops | bytes accessed | tf_op | source)
XLA Modules:
  0.0 14.9 jit_solution(16601856391100581140)
XLA Ops:
  0.0 14.2 %shard_map.46 = f32[32,256]{1,0:T(8,128)S(1)} custom-call(f32[16,256,256]{2,1,0:T(8,128)} %t_hbm.1, f32[32,256]{1,0:T(8,128)} %a_hbm.1, f32[16,256]{1,0:T(8,128)} %b_hbm.1, f32[16,16]{1,0:T(8,128)} %c_hbm.1), custom_call_target="tpu_custom_call" | custom-call | flops 402653184 | bytes 4194304 | tf_op jit(solution)/shard_map/pallas_call | solution.py:203
  14.3 0.6 %copy.6 = f32[32,256]{1,0:T(8,128)} copy(f32[32,256]{1,0:T(8,128)S(1)} %shard_map.46) | data formatting | bytes 65536

commit v10 on v9

--- a/solution.py
+++ b/solution.py
@@ -50,13 +50,14 @@
         pl.semaphore_signal(
             barrier, inc=1, device_id={"ia": lax.rem(ia + d, n_ia)}, device_id_type=MESH
         )
-    @pl.loop(1, n_red)
-    def _(d):
+    order = [*range(2, n_red), 1]
+    for d in order:
         peer = lax.rem(me + d, n_red)
         pl.semaphore_signal(
             barrier, inc=1, device_id={"ja": peer // n_ka, "ka": lax.rem(peer, n_ka)},
             device_id_type=MESH,
         )
+
     own = [
         pltpu.make_async_copy(b_hbm, b_all.at[ia], loc_sem.at[0]),
         pltpu.make_async_copy(c_hbm, c_all.at[ia], loc_sem.at[1]),
@@ -92,6 +93,7 @@
     sent = []
     for d in range(1, n_ia):
         sent += factors(lax.rem(ia + d, n_ia), ia, d - 1)
+    sent = sent[0::2] + sent[1::2]
     for d in range(1, n_ka):
         sent.append(ranks_a(lax.rem(ka + d, n_ka), ka, d - 1))
     for copy in sent:
@@ -138,15 +140,12 @@
             if h == 0:
                 high, low = th[:, columns], tl[:, columns]
             else:
-                high, low = split(
-                    jnp.concatenate(
-                        [
-                            t_v[k, :, h * hw : (h + 1) * hw]
-                            for k in range(g * step, (g + 1) * step)
-                        ],
-                        axis=1,
-                    )
-                )
+                pairs = [
+                    split(t_v[k, :, h * hw : (h + 1) * hw])
+                    for k in range(g * step, (g + 1) * step)
+                ]
+                high = jnp.concatenate([pair[0] for pair in pairs], axis=1)
+                low = jnp.concatenate([pair[1] for pair in pairs], axis=1)
             wide = dot(lhs, high)
             inner = wide[:ranks] + (wide[ranks:] + dot(bh, low))
             for u in range(step):
@@ -163,10 +162,8 @@
         for kk in range(n_ka):
             part[h, kk] = total[kk * ra : (kk + 1) * ra]
 
-        @pl.loop(1, n_red)
-        def _(d):
+        for d in order:
             exchange(h, d).start()
-
         recv[h, me] = part[h, ka]
 
     for copy in sent:
@@ -198,7 +195,7 @@
     halves = 2
     hw = il // halves
     n_red = n_ja * n_ka
-    groups = 4
+    groups = 8
     dma = pltpu.SemaphoreType.DMA
     return pl.pallas_call(
         functools.partial(kernel, n_ia, n_ja, n_ka, groups),

time: 15 us -> 15.6 us (1.040)
  Pallas kernels: 14.2 us -> 14.9 us
    pallas_call x1, Pallas kernels: 14.2 us -> 14.9 us  [local(): pl.pallas_call(functools.partial(kernel, n_ia, n_ja, n_ka, groups), out_s...]
where the time goes in v10:
time: 15.6 us; the launch traced here: 15.5 us
  Pallas kernels  14.9 us (96%)
  local copies, waits for them, and re-layouts  0.62 us (4%)
    pallas_call x1, Pallas kernels, local(): pl.pallas_call(functools.partial(kernel, n_ia, n_ja, n_ka, groups), out_s...  14.9 us
    unnamed x1, local copies, waits for them, and re-layouts  0.62 us

profile of v10, /device:TPU:0, one launch (start us, length us, event | category | flops | bytes accessed | tf_op | source)
XLA Modules:
  0.0 15.5 jit_solution(2069743818264446993)
XLA Ops:
  0.0 14.9 %shard_map.46 = f32[32,256]{1,0:T(8,128)S(1)} custom-call(f32[16,256,256]{2,1,0:T(8,128)} %t_hbm.1, f32[32,256]{1,0:T(8,128)} %a_hbm.1, f32[16,256]{1,0:T(8,128)} %b_hbm.1, f32[16,16]{1,0:T(8,128)} %c_hbm.1), custom_call_target="tpu_custom_call" | custom-call | flops 402653184 | bytes 4194304 | tf_op jit(solution)/shard_map/pallas_call | solution.py:200
  14.9 0.6 %copy.6 = f32[32,256]{1,0:T(8,128)} copy(f32[32,256]{1,0:T(8,128)S(1)} %shard_map.46) | data formatting | bytes 65536

commit v11 on v9

--- a/solution.py
+++ b/solution.py
@@ -62,13 +62,16 @@
         pltpu.make_async_copy(c_hbm, c_all.at[ia], loc_sem.at[1]),
         pltpu.make_async_copy(a_hbm, a_all.at[ka], loc_sem.at[2]),
     ]
-    loads = [
-        pltpu.make_async_copy(
-            t_hbm.at[pl.ds(g * step, step)], t_v.at[pl.ds(g * step, step)], t_sem.at[g]
-        )
-        for g in range(groups)
-    ]
-    for load in own + loads:
+    loads = []
+    for h in range(halves):
+        for g in range(groups):
+            place = (pl.ds(g * step, step), slice(None), pl.ds(h * hw, hw))
+            loads.append(
+                pltpu.make_async_copy(
+                    t_hbm.at[place], t_v.at[place], t_sem.at[h * groups + g]
+                )
+            )
+    for load in own + loads[:groups]:
         load.start()
     pl.semaphore_wait(barrier, n_ia - 1 + n_red - 1)
 
@@ -94,7 +97,7 @@
         sent += factors(lax.rem(ia + d, n_ia), ia, d - 1)
     for d in range(1, n_ka):
         sent.append(ranks_a(lax.rem(ka + d, n_ka), ka, d - 1))
-    for copy in sent:
+    for copy in sent + loads[groups:]:
         copy.start()
 
     for g in range(groups):
@@ -131,7 +134,9 @@
         )
 
     for h in range(halves):
-
+        if h > 0:
+            for load in loads[h * groups : (h + 1) * groups]:
+                load.wait()
         total = jnp.zeros((ranks, hw), F32)
         for g in range(groups):
             columns = pl.ds(g * step * hw, step * hw)
@@ -214,7 +219,7 @@
             pltpu.VMEM((n_ka, ra, il), F32),
             pltpu.VMEM((halves, n_ka, ra, hw), F32),
             pltpu.VMEM((halves, n_red, ra, hw), F32),
-            dma((groups,)),
+            dma((halves * groups,)),
             dma((3,)),
             dma((2, n_ia)),
             dma((2, n_ia)),

time: 15 us -> 15 us (level)
  no operation moved by 1% of the time
where the time goes in v11:
time: 15 us; the launch traced here: 14.9 us
  Pallas kernels  14.3 us (95%)
  local copies, waits for them, and re-layouts  0.62 us (4%)
    pallas_call x1, Pallas kernels, local(): pl.pallas_call(functools.partial(kernel, n_ia, n_ja, n_ka, groups), out_s...  14.3 us
    unnamed x1, local copies, waits for them, and re-layouts  0.62 us

profile of v11, /device:TPU:0, one launch (start us, length us, event | category | flops | bytes accessed | tf_op | source)
XLA Modules:
  0.0 14.9 jit_solution(10834736573739466608)
XLA Ops:
  0.0 14.3 %shard_map.46 = f32[32,256]{1,0:T(8,128)S(1)} custom-call(f32[16,256,256]{2,1,0:T(8,128)} %t_hbm.1, f32[32,256]{1,0:T(8,128)} %a_hbm.1, f32[16,256]{1,0:T(8,128)} %b_hbm.1, f32[16,16]{1,0:T(8,128)} %c_hbm.1), custom_call_target="tpu_custom_call" | custom-call | flops 402653184 | bytes 4194304 | tf_op jit(solution)/shard_map/pallas_call | solution.py:208
  14.3 0.6 %copy.6 = f32[32,256]{1,0:T(8,128)} copy(f32[32,256]{1,0:T(8,128)S(1)} %shard_map.46) | data formatting | bytes 65536

commit v12 on v9

--- a/solution.py
+++ b/solution.py
@@ -44,6 +44,7 @@
     n_red = n_ja * n_ka
     me = ja * n_ka + ka
     step = planes // groups
+    wide_step = 2 * step
 
     barrier = pltpu.get_barrier_semaphore()
     for d in range(1, n_ia):
@@ -133,8 +134,8 @@
     for h in range(halves):
 
         total = jnp.zeros((ranks, hw), F32)
-        for g in range(groups):
-            columns = pl.ds(g * step * hw, step * hw)
+        for g in range(planes // wide_step):
+            columns = pl.ds(g * wide_step * hw, wide_step * hw)
             if h == 0:
                 high, low = th[:, columns], tl[:, columns]
             else:
@@ -142,15 +143,15 @@
                     jnp.concatenate(
                         [
                             t_v[k, :, h * hw : (h + 1) * hw]
-                            for k in range(g * step, (g + 1) * step)
+                            for k in range(g * wide_step, (g + 1) * wide_step)
                         ],
                         axis=1,
                     )
                 )
             wide = dot(lhs, high)
             inner = wide[:ranks] + (wide[ranks:] + dot(bh, low))
-            for u in range(step):
-                k = g * step + u
+            for u in range(wide_step):
+                k = g * wide_step + u
                 total = total + inner[:, u * hw : (u + 1) * hw] * rank_c[:, k : k + 1]
 
             if h == 0 and g == 0:

time: 15 us -> 15 us (level)
  no operation moved by 1% of the time
where the time goes in v12:
time: 15 us; the launch traced here: 14.9 us
  Pallas kernels  14.3 us (95%)
  local copies, waits for them, and re-layouts  0.62 us (4%)
    pallas_call x1, Pallas kernels, local(): pl.pallas_call(functools.partial(kernel, n_ia, n_ja, n_ka, groups), out_s...  14.3 us
    unnamed x1, local copies, waits for them, and re-layouts  0.62 us

profile of v12, /device:TPU:0, one launch (start us, length us, event | category | flops | bytes accessed | tf_op | source)
XLA Modules:
  0.0 14.9 jit_solution(8219754745924907250)
XLA Ops:
  0.0 14.3 %shard_map.46 = f32[32,256]{1,0:T(8,128)S(1)} custom-call(f32[16,256,256]{2,1,0:T(8,128)} %t_hbm.1, f32[32,256]{1,0:T(8,128)} %a_hbm.1, f32[16,256]{1,0:T(8,128)} %b_hbm.1, f32[16,16]{1,0:T(8,128)} %c_hbm.1), custom_call_target="tpu_custom_call" | custom-call | flops 402653184 | bytes 4194304 | tf_op jit(solution)/shard_map/pallas_call | solution.py:204
  14.3 0.6 %copy.6 = f32[32,256]{1,0:T(8,128)} copy(f32[32,256]{1,0:T(8,128)S(1)} %shard_map.46) | data formatting | bytes 65536
